TPU v7x, 32 devices: a whole 2x2x4 slice. The times are simulated.
32 devices in a mesh: dp: 4 (over z), tensor: 8 (over y, x, core).
Axes of the slice: x: 2, y: 2, z: 4, core: 2. Of those that a mesh axis runs over, the one named last changes fastest.
Arguments:
- residues: bfloat16 [2048, 1024], P('dp'), may hold values from -40 to 40
- block_protein: int32 [16], P('dp'), may hold values from 0 to 15, as said below
- protein_length: int32 [16], replicated, may hold values from 0 to 256, as said below
- decoder_group: int32 [16], replicated, may hold values from 0 to 3, as said below
- enc_gain: float32 [1024], replicated, may hold values from 0.1 to 1.9
- enc_query: bfloat16 [1024, 8192], P(None, 'tensor'), may hold values from -2 to 2
- enc_key: bfloat16 [1024, 8192], P(None, 'tensor'), may hold values from -2 to 2
- enc_value: bfloat16 [1024, 8192], P(None, 'tensor'), may hold values from -0.1875 to 0.1875
- enc_out: bfloat16 [8192, 1024], P('tensor'), may hold values from -0.1875 to 0.1875
- decoder_states: bfloat16 [1536, 1024], P('dp'), may hold values from -40 to 40
- query_protein: int32 [1536], P('dp'), may hold values from 0 to 15, as said below
- dec_gain: float32 [1024], replicated, may hold values from 0.1 to 1.9
- final_gain: float32 [1024], replicated, may hold values from 0.1 to 1.9
- cross_query: bfloat16 [1024, 8192], P(None, 'tensor'), may hold values from -2 to 2
- cross_key: bfloat16 [1024, 8192], P(None, 'tensor'), may hold values from -2 to 2
- cross_value: bfloat16 [1024, 8192], P(None, 'tensor'), may hold values from -0.1875 to 0.1875
- cross_out: bfloat16 [8192, 1024], P('tensor'), may hold values from -0.1875 to 0.1875
Outputs:
- encoded: bfloat16 [2048, 1024], P('dp', 'tensor')
- decoded: bfloat16 [1536, 1024], P(('dp', 'tensor'))
Inputs may be any that keep to these rules, and one draw needn't show every extreme that they name: `block_protein`: block b of dp group d names a protein id from d * 4 to (d + 1) * 4 - 1; the blocks of one protein are consecutive and the ids rise along a group's blocks. `protein_length`: A protein of n blocks has a length from (n - 1) * 128 + 1 to n * 128; an id that no block names has length 0; no protein spans more than 2 blocks. `decoder_group`: at most 2 blocks of one dp group belong to proteins of one decoder group, and in every draw some decoder group gets exactly 2 blocks from every dp group; every decoder group owns a protein of positive length. `query_protein`: query row i names a protein of positive length whose decoder group is i // 384.
All inputs are finite; a program needn't handle non-finite values.
Results may differ from a plain program's by a relative error of at most 0.017.
Values may be sent and summed in bfloat16 or wider, within the bound.
A program may use at most 128 MiB of HBM per device.

v0:
```python
import jax
import jax.numpy as jnp
from jax import lax
from jax.sharding import PartitionSpec as P

HEAD_DIM = 128
BLOCK = 128


EPSILON = 1e-06
MASKED = -1000000000.0


def row_scale(matrix):
    values = matrix.astype(jnp.float32)
    return lax.rsqrt(jnp.mean(values * values, axis=1, keepdims=True) + EPSILON)


def table_lookup(indices, table):
    match = indices[:, None] == jnp.arange(table.shape[0], dtype=jnp.int32)[None, :]
    return jnp.sum(jnp.where(match, table[None, :], 0), axis=1)


def attend(queries, keys, values, allowed):
    count = queries.shape[0]
    heads = queries.shape[1] // HEAD_DIM
    query_heads = queries.reshape(count, heads, HEAD_DIM)
    key_heads = keys.reshape(keys.shape[0], heads, HEAD_DIM)
    value_heads = values.reshape(values.shape[0], heads, HEAD_DIM)
    scores = jnp.einsum(
        "qhd,khd->hqk", query_heads, key_heads, preferred_element_type=jnp.float32
    ) * HEAD_DIM ** (-0.5)
    scores = jnp.where(allowed[None], scores, MASKED)
    top = jnp.max(scores, axis=2, keepdims=True)
    expo = jnp.exp(scores - top)
    total = jnp.sum(expo, axis=2)
    weights = expo.astype(jnp.bfloat16)
    context = jnp.einsum("hqk,khd->qhd", weights, value_heads, preferred_element_type=jnp.float32)
    context = context / jnp.transpose(total)[:, :, None]
    return context.reshape(count, heads * HEAD_DIM).astype(jnp.bfloat16)


def body(
    residues,
    block_protein,
    protein_length,
    decoder_group,
    enc_gain,
    enc_query,
    enc_key,
    enc_value,
    enc_out,
    decoder_states,
    query_protein,
    dec_gain,
    final_gain,
    cross_query,
    cross_key,
    cross_value,
    cross_out,
):
    groups = lax.axis_size("dp")
    tensor_count = lax.axis_size("tensor")
    tensor_index = lax.axis_index("tensor")
    tok_rows = residues.shape[0]
    width = residues.shape[1]
    blocks = block_protein.shape[0]
    slots = blocks // 2
    order = jnp.arange(blocks, dtype=jnp.int32)
    same = block_protein[:, None] == block_protein[None, :]
    offset = jnp.sum(same & (order[None, :] < order[:, None]), axis=1)
    live = jnp.clip(table_lookup(block_protein, protein_length) - offset * BLOCK, 0, BLOCK)
    dest = table_lookup(block_protein, decoder_group)
    position = jnp.arange(BLOCK, dtype=jnp.int32)
    token_protein = jnp.broadcast_to(block_protein[:, None], (blocks, BLOCK)).reshape(tok_rows)
    token_valid = (position[None, :] < live[:, None]).reshape(tok_rows)
    normed = (residues.astype(jnp.float32) * row_scale(residues) * enc_gain[None, :]).astype(
        jnp.bfloat16
    )
    enc_queries = jnp.dot(normed, enc_query, preferred_element_type=jnp.float32).astype(
        jnp.bfloat16
    )
    enc_keys = jnp.dot(normed, enc_key, preferred_element_type=jnp.float32).astype(jnp.bfloat16)
    enc_values = jnp.dot(normed, enc_value, preferred_element_type=jnp.float32).astype(jnp.bfloat16)
    row_block = min(tok_rows, 512)
    block_count = tok_rows // row_block

    def encode_block(item):
        block_queries, block_owner = item
        permit = (block_owner[:, None] == token_protein[None, :]) & token_valid[None, :]
        return attend(block_queries, enc_keys, enc_values, permit)

    context = lax.map(
        encode_block,
        (
            enc_queries.reshape(block_count, row_block, -1),
            token_protein.reshape(block_count, row_block),
        ),
    )
    context = context.reshape(tok_rows, -1)
    partial_value = jnp.dot(context, enc_out, preferred_element_type=jnp.float32)
    slice_width = width // tensor_count
    column_start = tensor_index * slice_width
    same_dest = dest[:, None] == dest[None, :]
    rank = jnp.sum(same_dest & (order[None, :] < order[:, None]), axis=1)
    place = dest * slots + rank
    target = jnp.arange(groups * slots, dtype=jnp.int32)
    chosen = target[:, None] == place[None, :]
    occupied = jnp.any(chosen, axis=1)
    send_ids = jnp.where(
        occupied, jnp.sum(jnp.where(chosen, block_protein[None, :], 0), axis=1), -1
    )
    send_live = jnp.sum(jnp.where(chosen, live[None, :], 0), axis=1)
    send_meta = jnp.stack([send_ids, send_live], axis=-1).reshape(groups, slots, 2)
    shares = lax.psum_scatter(partial_value, "tensor", scatter_dimension=1, tiled=True)
    own_columns = lax.dynamic_slice_in_dim(residues, column_start, slice_width, 1)
    encoded = (own_columns.astype(jnp.float32) + shares).astype(jnp.bfloat16)
    features = encoded.shape[1]
    stacked = encoded.reshape(blocks, BLOCK * features)
    placed = jnp.dot(
        chosen.astype(jnp.bfloat16), stacked, preferred_element_type=jnp.float32
    ).astype(jnp.bfloat16)
    slice_grid = lax.all_to_all(
        placed.reshape(groups, slots, BLOCK, features),
        "dp",
        split_axis=0,
        concat_axis=0,
        tiled=True,
    )
    meta = lax.all_to_all(send_meta, "dp", split_axis=0, concat_axis=0, tiled=True)
    flat = slice_grid.reshape(-1, slice_width)
    inner = cross_key.shape[1]
    values32 = lax.all_gather(flat, "tensor", axis=1, tiled=True).astype(jnp.float32)
    scaled = (values32 * final_gain[None, :]).astype(jnp.bfloat16)
    key_sum = jnp.dot(scaled, cross_key, preferred_element_type=jnp.float32)
    value_sum = jnp.dot(scaled, cross_value, preferred_element_type=jnp.float32)
    squares = jnp.sum(values32 * values32, axis=1, keepdims=True)
    key_sum, value_sum, squares = (key_sum, value_sum, squares)
    key_scale = lax.rsqrt(squares / width + EPSILON)
    grid_shape = (groups, slots, BLOCK, inner)
    key_grid = (key_sum * key_scale).astype(jnp.bfloat16).reshape(grid_shape)
    value_grid = (value_sum * key_scale).astype(jnp.bfloat16).reshape(grid_shape)
    key_ids = meta[:, :, 0]
    key_live = meta[:, :, 1]
    key_valid = position[None, None, :] < key_live[:, :, None]
    query_rows = decoder_states.shape[0]
    dec_normed = (
        decoder_states.astype(jnp.float32) * row_scale(decoder_states) * dec_gain[None, :]
    ).astype(jnp.bfloat16)
    cross_queries = jnp.dot(dec_normed, cross_query, preferred_element_type=jnp.float32).astype(
        jnp.bfloat16
    )
    allowed = (query_protein[:, None, None, None] == key_ids[None, :, :, None]) & key_valid[None]
    slot_total = groups * slots
    inner_width = key_grid.shape[3]
    cross_context = attend(
        cross_queries,
        key_grid.reshape(slot_total * BLOCK, inner_width),
        value_grid.reshape(slot_total * BLOCK, inner_width),
        allowed.reshape(query_rows, slot_total * BLOCK),
    )
    share_rows = query_rows // tensor_count
    mixed = lax.psum_scatter(
        jnp.dot(cross_context, cross_out, preferred_element_type=jnp.float32).astype(jnp.bfloat16),
        "tensor",
        scatter_dimension=0,
        tiled=True,
    ).astype(jnp.float32)
    own_rows = lax.dynamic_slice_in_dim(decoder_states, tensor_index * share_rows, share_rows, 0)
    decoded = (own_rows.astype(jnp.float32) + mixed).astype(jnp.bfloat16)
    return (encoded, decoded)


def solution(mesh):
    in_specs = (
        P("dp", None),
        P("dp"),
        P(),
        P(),
        P(),
        P(None, "tensor"),
        P(None, "tensor"),
        P(None, "tensor"),
        P("tensor", None),
        P("dp", None),
        P("dp"),
        P(),
        P(),
        P(None, "tensor"),
        P(None, "tensor"),
        P(None, "tensor"),
        P("tensor", None),
    )
    out_specs = (P("dp", "tensor"), P(("dp", "tensor"), None))
    return jax.shard_map(body, mesh=mesh, in_specs=in_specs, out_specs=out_specs, check_vma=False)
```

profile of v0, /device:TPU:0, one launch (start us, length us, event | category | flops | bytes accessed | tf_op | source)
XLA Modules:
  0.0 184.1 jit_solution(16156888830326789966)
XLA Ops:
  7.2 0.0 reduce-scatter.3.cloned.1.call-start
  7.2 1.0 convert_reduce_fusion.1
  8.2 0.7 broadcast_bitcast_fusion
  8.9 0.9 select_reduce_fusion.2
  9.9 0.1 fusion.49
  9.9 1.5 fusion.17
  11.5 4.4 %fusion.31 = bf16[64,8,8,128]{3,2,1,0:T(8,128)(2,1)} fusion(bf16[1024,1024]{1,0:T(8,128)(2,1)} %param.22, bf16[512,1024]{1,0:T(8,128)(2,1)} %param.17, f32[1024]{0:T(1024)} %param.21, f32[512]{0:T(512)S(1)} %add_rsqrt_fusion.2), kind=kOutput, calls=%fused_computation.44 | convolution fusion | flops 1076363264 | bytes 4200448 | tf_op jit(solution)/shard_map/dot_general | solution.py:80
  15.9 2.3 %fusion.32 = bf16[64,8,8,128]{3,2,1,0:T(8,128)(2,1)} fusion(bf16[1024,1024]{1,0:T(8,128)(2,1)S(1)} %copy-done.11, bf16[512,1024]{1,0:T(8,128)(2,1)S(1)} %copy-done.4, f32[1024]{0:T(1024)S(1)} %copy-done.14, f32[512]{0:T(512)S(1)} %add_rsqrt_fusion.2), kind=kOutput, calls=%fused_computation.45 | convolution fusion | flops 1076363264 | bytes 4200448 | tf_op jit(solution)/shard_map/dot_general | solution.py:83
  18.2 2.3 %convolution_convert_fusion.3 = bf16[512,1024]{1,0:T(8,128)(2,1)} fusion(bf16[1024,1024]{1,0:T(8,128)(2,1)S(1)} %copy-done.12, bf16[512,1024]{1,0:T(8,128)(2,1)S(1)} %copy-done.4, f32[1024]{0:T(1024)S(1)} %copy-done.14, f32[512]{0:T(512)S(1)} %add_rsqrt_fusion.2), kind=kOutput, calls=%fused_computation.41 | convolution fusion | flops 1076363264 | bytes 4200448 | tf_op jit(solution)/shard_map/dot_general | solution.py:84
  20.5 2.3 %copy.66 = bf16[512,1024]{0,1:T(8,128)(2,1)} copy(bf16[512,1024]{1,0:T(8,128)(2,1)} %convolution_convert_fusion.3) | data formatting | bytes 2097152 | tf_op jit(solution)/shard_map/while/body/eval_jaxpr/reshape | solution.py:29
  22.8 0.2 compare_and_fusion
  23.0 3.2 %fusion.3 = (f32[8,512]{1,0:T(8,128)S(1)}, f32[8,512,512]{1,2,0:T(8,128)S(1)}) fusion(pred[512,512]{0,1:T(8,128)(4,1)S(1)} %compare_and_fusion, bf16[64,8,8,128]{3,2,1,0:T(8,128)(2,1)} %fusion.32, bf16[64,8,8,128]{3,2,1,0:T(8,128)(2,1)} %fusion.31), kind=kOutput, calls=%fused_computation.8 | convolution fusion | flops 543158272 | bytes 10764288 | tf_op jit(solution)/shard_map/while/body/eval_jaxpr/qhd,khd->hqk/dot_general | solution.py:30
  26.2 1.7 fusion.4
  28.0 2.6 %fusion.20 = bf16[512,8,128]{0,2,1:T(8,128)(2,1)S(1)} fusion(bf16[512,8,128]{0,2,1:T(8,128)(2,1)S(1)} %bitcast.65, f32[8,512,512]{1,2,0:T(8,128)S(1)} %get-tuple-element.33, f32[8,512]{1,0:T(8,128)S(1)} %get-tuple-element.32, pred[512,512]{0,1:T(8,128)(4,1)S(1)} %compare_and_fusion, f32[512,8]{0,1:T(8,128)S(1)} %bitcast.69), kind=kOutput, calls=%fused_computation.30 | convolution fusion | flops 546308096 | bytes 10780672 | tf_op jit(solution)/shard_map/while/body/eval_jaxpr/hqk,khd->qhd/dot_general | solution.py:38
  30.6 2.6 %fusion.59 = f32[512,1024]{1,0:T(8,128)} fusion(bf16[512,1024]{0,1:T(8,128)(2,1)S(1)} %bitcast.64, bf16[1024,1024]{1,0:T(8,128)(2,1)S(1)} %copy-done.2), kind=kOutput, calls=%fused_computation.91 | convolution fusion | flops 1073741824 | bytes 5242880 | tf_op jit(solution)/shard_map/dot_general | solution.py:101
  33.2 0.0 reduce-scatter.3.cloned.1.call-update
  33.2 0.0 all-gather.2.cloned.1.call-start
  33.3 0.2 convert_reduce_fusion
  33.5 43.8 %reduce-scatter.3.cloned.1.call-done = f32[512,128]{1,0:T(8,128)} async-done(((f32[512,1024]{1,0:T(8,128)}), f32[512,128]{1,0:T(8,128)}) %reduce-scatter.3.cloned.1.call-update) | async-done | bytes 262160 | tf_op jit(solution)/shard_map/reduce_scatter | solution.py:115
  77.3 1.0 add_convert_fusion
  78.4 0.3 fusion.34
  78.8 13.4 %all_to_all.10 = bf16[4,2,128,128]{3,2,1,0:T(8,128)(2,1)} all-to-all(bf16[4,2,128,128]{3,2,1,0:T(8,128)(2,1)S(1)} %bitcast.67), channel_id=1, replica_groups=mesh['dp'=4,'tensor'=8] {'dp'}, dimensions={0} | all-to-all | bytes 524288 | tf_op jit(solution)/shard_map/all_to_all | solution.py:123
  92.1 0.0 all-gather.2.cloned.1.call-update
  92.2 0.1 fusion.46
  92.3 0.1 select_reduce_fusion.1
  92.4 0.1 select_n.51
  92.4 0.1 stack.7
  92.5 0.6 copy.56
  93.1 3.2 %all-to-all-start.1 = ((s32[4,2,2]{1,2,0:T(2,128)}), s32[4,2,2]{1,2,0:T(2,128)S(1)}, u32[]{:S(2)}, u32[]{:S(2)}) async-start(s32[4,2,2]{1,2,0:T(2,128)} %copy.56), calls=%async_computation.2 | async-start | bytes 8192 | tf_op jit(solution)/shard_map/all_to_all | solution.py:130
  96.4 0.2 reduce-scatter.5.cloned.1.call-start
  96.6 0.2 fusion.25
  96.9 3.6 %fusion.33 = bf16[48,8,8,128]{3,2,1,0:T(8,128)(2,1)} fusion(bf16[1024,1024]{1,0:T(8,128)(2,1)} %param.30, bf16[384,1024]{1,0:T(8,128)(2,1)S(1)} %copy-done.6, f32[1024]{0:T(1024)S(1)} %copy-done.15, f32[384]{0:T(512)S(1)} %add_rsqrt_fusion.1), kind=kOutput, calls=%fused_computation.46 | convolution fusion | flops 807272448 | bytes 3675648 | tf_op jit(solution)/shard_map/dot_general | solution.py:150
  100.5 1.4 all-to-all-done.1
  101.9 0.1 iota_compare_fusion
  102.0 0.1 broadcast_compare_fusion
  102.1 0.2 bitcast_and_fusion
  102.4 0.6 copy.61
  102.9 15.7 %all-gather.2.cloned.1.call-done = bf16[1024,1024]{1,0:T(8,128)(2,1)} async-done(((bf16[1024,128]{1,0:T(8,128)(2,1)}), bf16[1024,1024]{1,0:T(8,128)(2,1)}) %all-gather.2.cloned.1.call-update) | async-done | bytes 2097168 | tf_op jit(solution)/shard_map/all_gather | solution.py:133
  118.6 2.2 %fusion.10 = f32[1024]{0:T(1024)S(1)} fusion(bf16[1024,1024]{1,0:T(8,128)(2,1)} %all-gather.2.cloned.1.call-done), kind=kLoop, calls=%fused_computation.16 | loop fusion | flops 3144704 | bytes 2101248 | tf_op jit(solution)/shard_map/reduce_sum | solution.py:137
  120.9 2.4 %multiply_convert_fusion = bf16[1024,1024]{0,1:T(8,128)(2,1)S(1)} fusion(bf16[1024,1024]{1,0:T(8,128)(2,1)S(1)} %copy-done, f32[1024]{0:T(1024)S(1)} %add_rsqrt_fusion, bf16[1024,1024]{1,0:T(8,128)(2,1)S(1)} %copy-done.3, f32[1024]{0:T(1024)S(1)} %copy-done.16), kind=kOutput, calls=%fused_computation.18 | convolution fusion | flops 2152726528 | bytes 6299648 | tf_op jit(solution)/shard_map/dot_general | solution.py:135
  123.4 2.7 %fusion = (f32[8,384]{1,0:T(8,128)S(1)}, f32[8,384,1024]{2,1,0:T(8,128)S(1)}) fusion(pred[384,1024]{1,0:T(8,128)(4,1)S(1)} %copy.61, bf16[1024,8,128]{0,2,1:T(8,128)(2,1)S(1)} %bitcast.63, bf16[48,8,8,128]{3,2,1,0:T(8,128)(2,1)S(1)} %copy-done.7), kind=kOutput, calls=%fused_computation.3 | convolution fusion | flops 814740480 | bytes 15872000 | tf_op jit(solution)/shard_map/qhd,khd->hqk/dot_general | solution.py:30
  126.1 3.6 %fusion.1 = f32[8,384]{1,0:T(8,128)S(1)} fusion(f32[8,384,1024]{2,1,0:T(8,128)S(1)} %get-tuple-element.35, f32[8,384]{1,0:T(8,128)S(1)} %get-tuple-element.34, pred[384,1024]{1,0:T(8,128)(4,1)S(1)} %copy.61), kind=kLoop, calls=%fused_computation.4 | loop fusion | flops 12579840 | bytes 13000704 | tf_op jit(solution)/shard_map/reduce_sum | solution.py:36
  129.7 3.8 %multiply_convert_fusion.1 = bf16[1024,1024]{0,1:T(8,128)(2,1)} fusion(bf16[1024,1024]{1,0:T(8,128)(2,1)S(1)} %copy-done.13, f32[1024]{0:T(1024)S(1)} %add_rsqrt_fusion, bf16[1024,1024]{1,0:T(8,128)(2,1)S(1)} %copy-done.3, f32[1024]{0:T(1024)S(1)} %copy-done.16), kind=kOutput, calls=%fused_computation.19 | convolution fusion | flops 2152726528 | bytes 6299648 | tf_op jit(solution)/shard_map/dot_general | solution.py:136
  133.5 5.4 %fusion.28 = bf16[384,8,128]{0,2,1:T(8,128)(2,1)S(1)} fusion(bf16[1024,8,128]{0,2,1:T(8,128)(2,1)} %bitcast.73, f32[8,384,1024]{2,1,0:T(8,128)S(1)} %get-tuple-element.35, f32[8,384]{1,0:T(8,128)S(1)} %get-tuple-element.34, pred[384,1024]{1,0:T(8,128)(4,1)S(1)} %copy.61, f32[384,8]{0,1:T(8,128)S(1)} %bitcast.70), kind=kOutput, calls=%fused_computation.37 | convolution fusion | flops 818675712 | bytes 15884288 | tf_op jit(solution)/shard_map/hqk,khd->qhd/dot_general | solution.py:38
  138.9 1.9 %convolution_convert_fusion.4 = bf16[384,1024]{1,0:T(8,128)(2,1)} fusion(bf16[384,1024]{0,1:T(8,128)(2,1)S(1)} %bitcast.68, bf16[1024,1024]{1,0:T(8,128)(2,1)S(1)} %copy-done.1), kind=kOutput, calls=%fused_computation.42 | convolution fusion | flops 805699584 | bytes 3670016 | tf_op jit(solution)/shard_map/dot_general | solution.py:164
  140.8 0.0 reduce-scatter.5.cloned.1.call-update
  140.8 35.1 %reduce-scatter.5.cloned.1.call-done = bf16[48,1024]{1,0:T(8,128)(2,1)} async-done(((bf16[384,1024]{1,0:T(8,128)(2,1)}), bf16[48,1024]{1,0:T(8,128)(2,1)}) %reduce-scatter.5.cloned.1.call-update) | async-done | bytes 98320 | tf_op jit(solution)/shard_map/reduce_scatter | solution.py:163
  175.9 1.6 add_convert_fusion.1
  (45 shorter events, 0.3 us)
Async XLA Ops:
  7.2 113.7 %copy-start = (bf16[1024,1024]{1,0:T(8,128)(2,1)S(1)}, bf16[1024,1024]{1,0:T(8,128)(2,1)}, u32[]{:S(2)}) copy-start(bf16[1024,1024]{1,0:T(8,128)(2,1)} %param.31) | copy-start | bytes 6291460
  7.2 70.1 %reduce-scatter.3.cloned.1.call-start = ((), (), s32[]{:S(2)}) async-start(), calls=%async_computation.4 | async-start | bytes 2359296 | tf_op jit(solution)/shard_map/reduce_scatter | solution.py:115
  11.4 4.4 %copy-start.4 = (bf16[512,1024]{1,0:T(8,128)(2,1)S(1)}, bf16[512,1024]{1,0:T(8,128)(2,1)}, u32[]{:S(2)}) copy-start(bf16[512,1024]{1,0:T(8,128)(2,1)} %param.17) | copy-start | bytes 3145732
  11.5 4.4 %copy-start.11 = (bf16[1024,1024]{1,0:T(8,128)(2,1)S(1)}, bf16[1024,1024]{1,0:T(8,128)(2,1)}, u32[]{:S(2)}) copy-start(bf16[1024,1024]{1,0:T(8,128)(2,1)} %param.23) | copy-start | bytes 6291460
  11.5 4.4 %copy-start.14 = (f32[1024]{0:T(1024)S(1)}, f32[1024]{0:T(1024)}, u32[]{:S(2)}) copy-start(f32[1024]{0:T(1024)} %param.21) | copy-start | bytes 12292
  15.9 2.3 %copy-start.12 = (bf16[1024,1024]{1,0:T(8,128)(2,1)S(1)}, bf16[1024,1024]{1,0:T(8,128)(2,1)}, u32[]{:S(2)}) copy-start(bf16[1024,1024]{1,0:T(8,128)(2,1)} %param.24) | copy-start | bytes 6291460
  26.2 1.8 copy-start.5
  28.0 2.6 %copy-start.2 = (bf16[1024,1024]{1,0:T(8,128)(2,1)S(1)}, bf16[1024,1024]{1,0:T(8,128)(2,1)}, u32[]{:S(2)}) copy-start(bf16[1024,1024]{1,0:T(8,128)(2,1)} %param.25) | copy-start | bytes 6291460
  33.2 59.0 %copy-start.9 = (s32[4]{0:T(128)S(1)}, s32[4]{0:T(128)}, u32[]{:S(2)}) copy-start(s32[4]{0:T(128)} %param.18) | copy-start | bytes 52
  33.2 63.6 %copy-start.15 = (f32[1024]{0:T(1024)S(1)}, f32[1024]{0:T(1024)}, u32[]{:S(2)}) copy-start(f32[1024]{0:T(1024)} %param.28) | copy-start | bytes 12292
  33.2 85.4 %all-gather.2.cloned.1.call-start = ((), (), s32[]{:S(2)}) async-start(), calls=%async_computation.5 | async-start | bytes 2359296 | tf_op jit(solution)/shard_map/all_gather | solution.py:133
  78.3 22.2 %copy-start.8 = (bf16[512,128]{1,0:T(8,128)(2,1)}, bf16[512,128]{1,0:T(8,128)(2,1)S(1)}, u32[]{:S(2)}) copy-start(bf16[512,128]{1,0:T(8,128)(2,1)S(1)} %add_convert_fusion) | copy-start | bytes 393220
  78.3 18.3 %copy-start.6 = (bf16[384,1024]{1,0:T(8,128)(2,1)S(1)}, bf16[384,1024]{1,0:T(8,128)(2,1)}, u32[]{:S(2)}) copy-start(bf16[384,1024]{1,0:T(8,128)(2,1)} %param.26) | copy-start | bytes 2359300
  93.1 8.8 %all-to-all-start.1 = ((s32[4,2,2]{1,2,0:T(2,128)}), s32[4,2,2]{1,2,0:T(2,128)S(1)}, u32[]{:S(2)}, u32[]{:S(2)}) async-start(s32[4,2,2]{1,2,0:T(2,128)} %copy.56), calls=%async_computation.2 | async-start | bytes 8192 | tf_op jit(solution)/shard_map/all_to_all | solution.py:130
  96.4 79.5 %reduce-scatter.5.cloned.1.call-start = ((), (), s32[]{:S(2)}) async-start(), calls=%async_computation.6 | async-start | bytes 884736 | tf_op jit(solution)/shard_map/reduce_scatter | solution.py:163
  96.9 5.2 %copy-start.10 = (s32[384]{0:T(512)S(1)}, s32[384]{0:T(512)}, u32[]{:S(2)}) copy-start(s32[384]{0:T(512)} %param.27) | copy-start | bytes 4612
  100.5 20.4 %copy-start.16 = (f32[1024]{0:T(1024)S(1)}, f32[1024]{0:T(1024)}, u32[]{:S(2)}) copy-start(f32[1024]{0:T(1024)} %param.29) | copy-start | bytes 12292
  118.6 2.3 %copy-start.3 = (bf16[1024,1024]{1,0:T(8,128)(2,1)S(1)}, bf16[1024,1024]{1,0:T(8,128)(2,1)}, u32[]{:S(2)}) copy-start(bf16[1024,1024]{1,0:T(8,128)(2,1)} %all-gather.2.cloned.1.call-done) | copy-start | bytes 6291460
  120.9 2.4 %copy-start.7 = (bf16[48,8,8,128]{3,2,1,0:T(8,128)(2,1)S(1)}, bf16[48,8,8,128]{3,2,1,0:T(8,128)(2,1)}, u32[]{:S(2)}) copy-start(bf16[48,8,8,128]{3,2,1,0:T(8,128)(2,1)} %fusion.33) | copy-start | bytes 2359300
  126.0 3.6 %copy-start.13 = (bf16[1024,1024]{1,0:T(8,128)(2,1)S(1)}, bf16[1024,1024]{1,0:T(8,128)(2,1)}, u32[]{:S(2)}) copy-start(bf16[1024,1024]{1,0:T(8,128)(2,1)} %param.32) | copy-start | bytes 6291460
  133.5 5.4 %copy-start.1 = (bf16[1024,1024]{1,0:T(8,128)(2,1)S(1)}, bf16[1024,1024]{1,0:T(8,128)(2,1)}, u32[]{:S(2)}) copy-start(bf16[1024,1024]{1,0:T(8,128)(2,1)} %param.33) | copy-start | bytes 6291460
Sparse Core Ops, SparseCore 0:
  33.4 43.9 reduce-scatter.2
  92.3 26.3 all-gather.1
  140.9 34.9 reduce-scatter.4
where the time goes:
time: 185 us; the launch traced here: 184 us
  waiting for transfers between devices  96.1 us (52%)
  matrix products  37.5 us (20%)
  other arithmetic  14.9 us (8%)
  between operations  14.1 us (8%)
  blocking collectives  13.4 us (7%)
  local copies, waits for them, and re-layouts  4.56 us (2%)
  starting transfers between devices  3.55 us (2%)
    reduce_scatter x1, waiting for transfers between devices, body(): lax.psum_scatter(partial_value, 'tensor', scatter_dimension=1, tiled=True)  43.8 us
    reduce_scatter x1, waiting for transfers between devices, body(): lax.psum_scatter(jnp.dot(cross_context, cross_out, preferred_element_type...  35.1 us
    all_gather x1, waiting for transfers between devices, body(): lax.all_gather(flat, 'tensor', axis=1, tiled=True).astype(jnp.float32)  15.7 us
    all_to_all x1, blocking collectives, body(): lax.all_to_all(placed.reshape(groups, slots, BLOCK, features), 'dp', spli...  13.4 us
    dot_general x2, matrix products, attend(): jnp.einsum('hqk,khd->qhd', weights, value_heads, preferred_element_type=j...  7.94 us
    dot_general x2, matrix products, attend(): jnp.einsum('qhd,khd->hqk', query_heads, key_heads, preferred_element_type...  5.88 us
    reduce_sum x2, other arithmetic, attend(): total = jnp.sum(expo, axis=2)  5.35 us
    dot_general x1, matrix products, body(): jnp.dot(normed, enc_query, preferred_element_type=jnp.float32)  4.41 us
  transfers between devices with their start and end apart: 4, of which 4 were waited for; matrix products, arithmetic and copies ran while one was open for 3% of the time, Pallas kernels for 0%

commit v1 on v0

v1 whole, which is shorter than its diff:
```python
import functools

import jax
import jax.numpy as jnp
from jax import lax
from jax.experimental import pallas as pl
from jax.experimental.pallas import tpu as pltpu
from jax.sharding import PartitionSpec as P

HEAD_DIM = 128
BLOCK = 128
LANES = 128

EPSILON = 1e-06
LOG2E = 1.4426950408889634
MASKED = -1000000000.0
SCORE_SCALE = HEAD_DIM ** (-0.5)
RAW_MASKED = MASKED / SCORE_SCALE
MESH = pl.DeviceIdType.MESH
F32 = jnp.float32
BF16 = jnp.bfloat16


def normalise(source, gain, target, rows):
    for start in range(0, source.shape[0], rows):
        values = source[start : start + rows, :].astype(F32)
        scale = lax.rsqrt(jnp.mean(values * values, axis=1, keepdims=True) + EPSILON)
        target[start : start + rows, :] = (values * scale * gain[...]).astype(BF16)


def project(source, weight, target, tile=256):
    @pl.loop(0, weight.shape[1] // tile)
    def _(index):
        columns = pl.ds(pl.multiple_of(index * tile, tile), tile)
        target[:, columns] = jnp.dot(
            source[...], weight[:, columns], preferred_element_type=F32
        ).astype(BF16)


def attend(queries, keys, values, bias, context, q_rows, k_rows, heads, together=2):
    @pl.loop(0, heads // together)
    def _(index):
        for inner in range(together):
            start = pl.multiple_of((index * together + inner) * HEAD_DIM, HEAD_DIM)
            columns = pl.ds(start, HEAD_DIM)
            scores = lax.dot_general(
                queries[q_rows, columns],
                keys[k_rows, columns],
                (((1,), (1,)), ((), ())),
                preferred_element_type=F32,
            )
            scores = scores + bias[...]
            top = jnp.max(scores, axis=1, keepdims=True)
            expo = jnp.exp2((scores - top) * (SCORE_SCALE * LOG2E))
            total = jnp.sum(expo, axis=1, keepdims=True)
            mixed = jnp.dot(
                expo.astype(BF16), values[k_rows, columns], preferred_element_type=F32
            )
            context[q_rows, columns] = (mixed / total).astype(BF16)


def kernel(
    groups,
    tensors,
    residues,
    block_protein,
    protein_length,
    decoder_group,
    enc_gain,
    enc_query,
    enc_key,
    enc_value,
    enc_out,
    decoder_states,
    query_protein,
    dec_gain,
    final_gain,
    cross_query,
    cross_key,
    cross_value,
    cross_out,
    encoded,
    decoded,
    res_v,
    dec_v,
    w_eq,
    w_ek,
    w_ev,
    w_eo,
    w_cq,
    w_ck,
    w_cv,
    w_co,
    normed,
    e_q,
    e_k,
    e_v,
    e_ctx,
    e_bias,
    part,
    rx1,
    tx2,
    rx2,
    placed,
    gath,
    meta_tx,
    meta_rx,
    d_normed,
    c_q,
    c_k,
    c_v,
    c_ctx,
    c_bias,
    scaled,
    dpart,
    drx1,
    dtx2,
    drx2,
    load_sem,
    meta_sem,
    rs1_sem,
    rs2_sem,
    a2a_sem,
    ag_sem,
    agp_sem,
    drs1_sem,
    drs2_sem,
):
    me_dp = lax.axis_index("dp")
    me_t = lax.axis_index("tensor")
    pairs = tensors // 2
    pair = me_t // 2
    side = lax.rem(me_t, 2)
    partner = pair * 2 + (1 - side)
    tok_rows, width = res_v.shape
    blocks = tok_rows // BLOCK
    slots = blocks // 2
    heads = e_q.shape[1] // HEAD_DIM
    half = tok_rows // 2
    half_blocks = blocks // 2
    share = encoded.shape[1]
    query_rows = dec_v.shape[0]
    row_share = query_rows // tensors
    row_pad = dpart.shape[3]

    def peer(step):
        return lax.rem(pair + step, pairs) * 2 + side

    loads = []
    for index, (src, dst) in enumerate(
        (
            (residues, res_v),
            (enc_query, w_eq),
            (enc_key, w_ek),
            (enc_value, w_ev),
            (enc_out, w_eo),
            (decoder_states, dec_v),
            (cross_query, w_cq),
            (cross_key, w_ck),
            (cross_value, w_cv),
            (cross_out, w_co),
        )
    ):
        load = pltpu.make_async_copy(src, dst, load_sem.at[index])
        load.start()
        loads.append(load)

    barrier = pltpu.get_barrier_semaphore()
    pl.semaphore_signal(barrier, inc=1, device_id={"tensor": partner}, device_id_type=MESH)
    for step in range(1, pairs):
        pl.semaphore_signal(
            barrier, inc=1, device_id={"tensor": peer(step)}, device_id_type=MESH
        )
    for step in range(1, groups):
        pl.semaphore_signal(
            barrier,
            inc=1,
            device_id={"dp": lax.rem(me_dp + step, groups)},
            device_id_type=MESH,
        )

    sent = []

    def send(src, dst, sems, device):
        copy = pltpu.make_async_remote_copy(
            src_ref=src,
            dst_ref=dst,
            send_sem=sems[0],
            recv_sem=sems[1],
            device_id=device,
            device_id_type=MESH,
        )
        copy.start()
        sent.append(copy)

    def arrive(dst, sems, device):
        pltpu.make_async_remote_copy(
            src_ref=dst,
            dst_ref=dst,
            send_sem=sems[0],
            recv_sem=sems[1],
            device_id=device,
            device_id_type=MESH,
        ).wait_recv()

    owner = [block_protein[b] for b in range(blocks)]
    live, dest, rank = [], [], []
    for b in range(blocks):
        offset = jnp.int32(0)
        for other in range(b):
            offset = offset + jnp.where(owner[other] == owner[b], 1, 0)
        length = protein_length[owner[b]]
        live.append(jnp.clip(length - offset * BLOCK, 0, BLOCK))
        dest.append(decoder_group[owner[b]])
    for b in range(blocks):
        place = jnp.int32(0)
        for other in range(b):
            place = place + jnp.where(dest[other] == dest[b], 1, 0)
        rank.append(place)

    lane = lax.broadcasted_iota(jnp.int32, (8, LANES), 1)
    row = lax.broadcasted_iota(jnp.int32, (8, LANES), 0)
    for g in range(groups):
        ids = jnp.full((8, LANES), -1, jnp.int32)
        for s in range(slots):
            slot_id, slot_live = jnp.int32(-1), jnp.int32(0)
            for b in range(blocks):
                match = (dest[b] == g) & (rank[b] == s)
                slot_id = jnp.where(match, owner[b], slot_id)
                slot_live = jnp.where(match, live[b], slot_live)
            row_live = jnp.where(row == s, slot_live, 0)
            ids = jnp.where(lane < row_live, slot_id, ids)
        meta_tx[g] = ids

    pl.semaphore_wait(barrier, 1 + (pairs - 1) + (groups - 1))
    for step in range(1, groups):
        target = lax.rem(me_dp + step, groups)
        send(
            meta_tx.at[target],
            meta_rx.at[groups - step],
            (meta_sem.at[0, step], meta_sem.at[1, groups - step]),
            {"dp": target},
        )
    meta_rx[0] = meta_tx[me_dp]

    loads[0].wait()
    normalise(res_v, enc_gain, normed, BLOCK)
    for index, (weight, target) in enumerate(((w_eq, e_q), (w_ek, e_k), (w_ev, e_v))):
        loads[1 + index].wait()
        project(normed, weight, target)

    block_lane = lax.broadcasted_iota(jnp.int32, (BLOCK, BLOCK), 1)

    def second_stage(r):
        arrive(rx1.at[r], (rs1_sem.at[0, r], rs1_sem.at[1, r]), {"tensor": partner})
        for step in range(1, pairs):
            target = lax.rem(pair + step, pairs)
            tx2[r, step - 1] = (
                part[r, side, target].astype(F32) + rx1[r, target].astype(F32)
            ).astype(BF16)
            send(
                tx2.at[r, step - 1],
                rx2.at[r, step - 1],
                (rs2_sem.at[0, r, step - 1], rs2_sem.at[1, r, step - 1]),
                {"tensor": peer(step)},
            )

    for r in range(2):
        first, last = r * half_blocks, (r + 1) * half_blocks
        key_first, key_last = max(first - 1, 0), min(last + 1, blocks)
        for b in range(first, last):
            for kb in range(key_first, key_last):
                seen = jnp.where(owner[b] == owner[kb], live[kb], 0)
                e_bias[
                    r,
                    (b - first) * BLOCK : (b - first + 1) * BLOCK,
                    (kb - key_first) * BLOCK : (kb - key_first + 1) * BLOCK,
                ] = jnp.where(block_lane < seen, 0.0, RAW_MASKED)
        key_count = (key_last - key_first) * BLOCK
        attend(
            e_q,
            e_k,
            e_v,
            e_bias.at[r, :, pl.ds(0, key_count)],
            e_ctx,
            pl.ds(r * half, half),
            pl.ds(key_first * BLOCK, key_count),
            heads,
        )
        if r == 0:
            loads[4].wait()
        tile = max(256, share)
        per_tile = tile // share
        for index in range(width // tile):
            sums = jnp.dot(
                e_ctx[r * half : (r + 1) * half, :],
                w_eo[:, index * tile : (index + 1) * tile],
                preferred_element_type=F32,
            )
            for inner in range(per_tile):
                j = index * per_tile + inner
                part[r, j % 2, j // 2] = sums[:, inner * share : (inner + 1) * share].astype(
                    BF16
                )
        send(
            part.at[r, 1 - side],
            rx1.at[r],
            (rs1_sem.at[0, r], rs1_sem.at[1, r]),
            {"tensor": partner},
        )
        if r == 0:
            loads[5].wait()
            normalise(dec_v, dec_gain, d_normed, BLOCK)
            second_stage(0)
    loads[6].wait()
    project(d_normed, w_cq, c_q)
    second_stage(1)

    for step in range(1, groups):
        arrive(
            meta_rx.at[step],
            (meta_sem.at[0, step], meta_sem.at[1, step]),
            {"dp": me_dp},
        )
    for q in range(query_rows // LANES):
        wanted = jnp.broadcast_to(
            query_protein[q : q + 1, :].astype(F32), (LANES, LANES)
        ).T
        for g in range(groups):
            for s in range(slots):
                named = meta_rx[g, s : s + 1, :].astype(F32)
                start = (g * slots + s) * BLOCK
                c_bias[q * LANES : (q + 1) * LANES, start : start + BLOCK] = jnp.where(
                    wanted == named, 0.0, RAW_MASKED
                )

    for r in range(2):
        rows = slice(r * half, (r + 1) * half)
        if share % LANES == 0:
            own = res_v[rows, pl.ds(pl.multiple_of(me_t * share, LANES), share)].astype(F32)
        else:
            own = jnp.zeros((half, share), F32)
            for j in range(tensors):
                mine = jnp.where(me_t == j, 1.0, 0.0)
                own = own + mine * res_v[rows, j * share : (j + 1) * share].astype(F32)
        sums = part[r, side, pair].astype(F32) + rx1[r, pair].astype(F32)
        for step in range(1, pairs):
            arrive(
                rx2.at[r, step - 1],
                (rs2_sem.at[0, r, step - 1], rs2_sem.at[1, r, step - 1]),
                {"tensor": partner},
            )
            sums = sums + rx2[r, step - 1].astype(F32)
        encoded[rows, :] = (own + sums).astype(BF16)

    for g in range(groups):
        for s in range(slots):
            block = jnp.zeros((BLOCK, share), F32)
            for b in range(blocks):
                match = (dest[b] == g) & (rank[b] == s)
                chosen = jnp.where(match, 1.0, 0.0)
                block = block + chosen * encoded[b * BLOCK : (b + 1) * BLOCK, :].astype(F32)
            placed[g, s * BLOCK : (s + 1) * BLOCK, :] = block.astype(BF16)
    for step in range(1, groups):
        target = lax.rem(me_dp + step, groups)
        send(
            placed.at[target],
            gath.at[groups - step, me_t],
            (a2a_sem.at[0, step], a2a_sem.at[1, groups - step]),
            {"dp": target},
        )
    gath[0, me_t] = placed[me_dp]

    def begin(g):
        if g > 0:
            arrive(
                gath.at[g, me_t], (a2a_sem.at[0, g], a2a_sem.at[1, g]), {"dp": me_dp}
            )
        for step in range(1, pairs):
            send(
                gath.at[g, me_t],
                gath.at[g, me_t],
                (ag_sem.at[0, g, step], ag_sem.at[1, g, step]),
                {"tensor": peer(step)},
            )
        send(
            gath.at[g, me_t],
            gath.at[g, me_t],
            (agp_sem.at[0, g, 0], agp_sem.at[1, g, 0]),
            {"tensor": partner},
        )

    def forward(g):
        for step in range(1, pairs):
            origin = lax.rem(pair + pairs - step, pairs) * 2 + side
            arrive(
                gath.at[g, origin],
                (ag_sem.at[0, g, step], ag_sem.at[1, g, step]),
                {"tensor": partner},
            )
            send(
                gath.at[g, origin],
                gath.at[g, origin],
                (agp_sem.at[0, g, step], agp_sem.at[1, g, step]),
                {"tensor": partner},
            )

    slot_rows = slots * BLOCK

    def keys_values(g):
        for step in range(pairs):
            origin = lax.rem(pair + pairs - step, pairs) * 2 + (1 - side)
            arrive(
                gath.at[g, origin],
                (agp_sem.at[0, g, step], agp_sem.at[1, g, step]),
                {"tensor": partner},
            )
        squares = jnp.zeros((slot_rows, 1), F32)
        for j in range(tensors):
            values = gath[g, j].astype(F32)
            squares = squares + jnp.sum(values * values, axis=1, keepdims=True)
            scaled[:, j * share : (j + 1) * share] = (
                values * final_gain[:, j * share : (j + 1) * share]
            ).astype(BF16)
        key_scale = lax.rsqrt(squares / width + EPSILON)
        rows = pl.ds(g * slot_rows, slot_rows)
        for weight, target in ((w_ck, c_k), (w_cv, c_v)):

            @pl.loop(0, weight.shape[1] // 256)
            def _(index):
                columns = pl.ds(pl.multiple_of(index * 256, 256), 256)
                sums = jnp.dot(scaled[...], weight[:, columns], preferred_element_type=F32)
                target[rows, columns] = (sums * key_scale).astype(BF16)

    loads[7].wait()
    loads[8].wait()
    begin(0)
    for g in range(1, groups + 2):
        if g < groups:
            begin(g)
        if g - 1 < groups:
            forward(g - 1)
        if g >= 2:
            keys_values(g - 2)

    attend(
        c_q,
        c_k,
        c_v,
        c_bias,
        c_ctx,
        pl.ds(0, query_rows),
        pl.ds(0, groups * slot_rows),
        heads,
        2 if groups * slot_rows <= 1024 else 1,
    )

    loads[9].wait()
    half_width = width // 2

    def decoder_stage(r):
        arrive(drx1.at[r], (drs1_sem.at[0, r], drs1_sem.at[1, r]), {"tensor": partner})
        for step in range(1, pairs):
            target = lax.rem(pair + step, pairs)
            dtx2[r, step - 1] = (
                dpart[r, side, target].astype(F32) + drx1[r, target].astype(F32)
            ).astype(BF16)
            send(
                dtx2.at[r, step - 1],
                drx2.at[r, step - 1],
                (drs2_sem.at[0, r, step - 1], drs2_sem.at[1, r, step - 1]),
                {"tensor": peer(step)},
            )

    for r in range(2):
        for index in range(half_width // 256):
            start = r * half_width + index * 256
            sums = jnp.dot(
                c_ctx[...], w_co[:, start : start + 256], preferred_element_type=F32
            )
            for j in range(tensors):
                piece = sums[j * row_share : (j + 1) * row_share, :]
                if row_pad > row_share:
                    piece = jnp.concatenate(
                        [piece, jnp.zeros((row_pad - row_share, 256), F32)], axis=0
                    )
                dpart[r, j % 2, j // 2, :, index * 256 : (index + 1) * 256] = piece.astype(
                    BF16
                )
        send(
            dpart.at[r, 1 - side],
            drx1.at[r],
            (drs1_sem.at[0, r], drs1_sem.at[1, r]),
            {"tensor": partner},
        )
    decoder_stage(0)
    decoder_stage(1)
    for r in range(2):
        columns = slice(r * half_width, (r + 1) * half_width)
        if row_share % 16 == 0:
            own = dec_v[pl.ds(pl.multiple_of(me_t * row_share, 16), row_share), columns]
            own = own.astype(F32)
        else:
            own = jnp.zeros((row_share, half_width), F32)
            everything = dec_v[:, columns].astype(F32)
            for j in range(tensors):
                mine = jnp.where(me_t == j, 1.0, 0.0)
                own = own + mine * everything[j * row_share : (j + 1) * row_share, :]
        sums = dpart[r, side, pair].astype(F32) + drx1[r, pair].astype(F32)
        for step in range(1, pairs):
            arrive(
                drx2.at[r, step - 1],
                (drs2_sem.at[0, r, step - 1], drs2_sem.at[1, r, step - 1]),
                {"tensor": partner},
            )
            sums = sums + drx2[r, step - 1].astype(F32)
        decoded[:, columns] = (own + sums[:row_share, :]).astype(BF16)

    for copy in sent:
        copy.wait_send()


def body(groups, tensors, *args):
    (
        residues,
        block_protein,
        protein_length,
        decoder_group,
        enc_gain,
        enc_query,
        enc_key,
        enc_value,
        enc_out,
        decoder_states,
        query_protein,
        dec_gain,
        final_gain,
        cross_query,
        cross_key,
        cross_value,
        cross_out,
    ) = args
    tok_rows, width = residues.shape
    query_rows = decoder_states.shape[0]
    inner = enc_query.shape[1]
    blocks = tok_rows // BLOCK
    slots = blocks // 2
    slot_rows = slots * BLOCK
    pairs = tensors // 2
    half = tok_rows // 2
    share = width // tensors
    row_share = query_rows // tensors
    row_pad = -(-row_share // 16) * 16
    keys = groups * slot_rows
    key_span = min(blocks, blocks // 2 + 1) * BLOCK
    hbm = pl.BlockSpec(memory_space=pl.ANY)
    smem = pl.BlockSpec(memory_space=pltpu.SMEM)
    vmem = pl.BlockSpec(memory_space=pltpu.VMEM)
    weight = pltpu.VMEM((width, inner), BF16)
    out_weight = pltpu.VMEM((inner, width), BF16)
    dma = pltpu.SemaphoreType.DMA
    return pl.pallas_call(
        functools.partial(kernel, groups, tensors),
        out_shape=(
            jax.ShapeDtypeStruct((tok_rows, share), BF16),
            jax.ShapeDtypeStruct((row_share, width), BF16),
        ),
        in_specs=[
            hbm,
            smem,
            smem,
            smem,
            vmem,
            hbm,
            hbm,
            hbm,
            hbm,
            hbm,
            vmem,
            vmem,
            vmem,
            hbm,
            hbm,
            hbm,
            hbm,
        ],
        out_specs=(vmem, vmem),
        scratch_shapes=[
            pltpu.VMEM((tok_rows, width), BF16),
            pltpu.VMEM((query_rows, width), BF16),
            weight,
            weight,
            weight,
            out_weight,
            weight,
            weight,
            weight,
            out_weight,
            pltpu.VMEM((tok_rows, width), BF16),
            pltpu.VMEM((tok_rows, inner), BF16),
            pltpu.VMEM((tok_rows, inner), BF16),
            pltpu.VMEM((tok_rows, inner), BF16),
            pltpu.VMEM((tok_rows, inner), BF16),
            pltpu.VMEM((2, half, key_span), F32),
            pltpu.VMEM((2, 2, pairs, half, share), BF16),
            pltpu.VMEM((2, pairs, half, share), BF16),
            pltpu.VMEM((2, pairs - 1, half, share), BF16),
            pltpu.VMEM((2, pairs - 1, half, share), BF16),
            pltpu.VMEM((groups, slot_rows, share), BF16),
            pltpu.VMEM((groups, tensors, slot_rows, share), BF16),
            pltpu.VMEM((groups, 8, LANES), jnp.int32),
            pltpu.VMEM((groups, 8, LANES), jnp.int32),
            pltpu.VMEM((query_rows, width), BF16),
            pltpu.VMEM((query_rows, inner), BF16),
            pltpu.VMEM((keys, inner), BF16),
            pltpu.VMEM((keys, inner), BF16),
            pltpu.VMEM((query_rows, inner), BF16),
            pltpu.VMEM((query_rows, keys), F32),
            pltpu.VMEM((slot_rows, width), BF16),
            pltpu.VMEM((2, 2, pairs, row_pad, width // 2), BF16),
            pltpu.VMEM((2, pairs, row_pad, width // 2), BF16),
            pltpu.VMEM((2, pairs - 1, row_pad, width // 2), BF16),
            pltpu.VMEM((2, pairs - 1, row_pad, width // 2), BF16),
            dma((10,)),
            dma((2, groups)),
            dma((2, 2)),
            dma((2, 2, pairs - 1)),
            dma((2, groups)),
            dma((2, groups, pairs)),
            dma((2, groups, pairs)),
            dma((2, 2)),
            dma((2, 2, pairs - 1)),
        ],
        compiler_params=pltpu.CompilerParams(
            collective_id=0,
            has_side_effects=True,
            vmem_limit_bytes=60 * 1024 * 1024,
        ),
    )(
        residues,
        block_protein,
        protein_length,
        decoder_group,
        enc_gain.reshape(1, width),
        enc_query,
        enc_key,
        enc_value,
        enc_out,
        decoder_states,
        query_protein.reshape(query_rows // LANES, LANES),
        dec_gain.reshape(1, width),
        final_gain.reshape(1, width),
        cross_query,
        cross_key,
        cross_value,
        cross_out,
    )


def solution(mesh):
    in_specs = (
        P("dp", None),
        P("dp"),
        P(),
        P(),
        P(),
        P(None, "tensor"),
        P(None, "tensor"),
        P(None, "tensor"),
        P("tensor", None),
        P("dp", None),
        P("dp"),
        P(),
        P(),
        P(None, "tensor"),
        P(None, "tensor"),
        P(None, "tensor"),
        P("tensor", None),
    )
    out_specs = (P("dp", "tensor"), P(("dp", "tensor"), None))
    return jax.shard_map(
        functools.partial(body, mesh.shape["dp"], mesh.shape["tensor"]),
        mesh=mesh,
        in_specs=in_specs,
        out_specs=out_specs,
        check_vma=False,
    )
```

time: 185 us -> 72.8 us (0.39)
  waiting for transfers between devices: 96.1 us -> 0 us
  Pallas kernels: 0 us -> 68.9 us
  matrix products: 37.5 us -> 0 us
  other arithmetic: 14.9 us -> 0 us
  between operations: 14.1 us -> 0.65 us
  blocking collectives: 13.4 us -> 0 us
  starting transfers between devices: 3.55 us -> 0 us
    reduce_scatter x2 -> x0, waiting for transfers between devices: 79 us -> none  [the longest x1 43.8 us: body(): lax.psum_scatter(partial_value, 'tensor', scatter_dimension=1, tiled=True)]
    pallas_call x0 -> x1, Pallas kernels: none -> 68.9 us  [body(): pl.pallas_call(functools.partial(kernel, groups, tensors), out_shape=(jax...]
    dot_general x13 -> x0, matrix products: 37.5 us -> none  [the longest x2 7.94 us: attend(): jnp.einsum('hqk,khd->qhd', weights, value_heads, preferred_element_type=j...]
    all_gather x1 -> x0, waiting for transfers between devices: 15.7 us -> none  [body(): lax.all_gather(flat, 'tensor', axis=1, tiled=True).astype(jnp.float32)]
    all_to_all x1 -> x0, blocking collectives: 13.4 us -> none  [body(): lax.all_to_all(placed.reshape(groups, slots, BLOCK, features), 'dp', spli...]
    reduce_sum x9 -> x0, other arithmetic: 11.5 us -> none  [the longest x2 5.35 us: attend(): total = jnp.sum(expo, axis=2)]
    all_to_all x1 -> x0, starting transfers between devices: 3.25 us -> none  [body(): lax.all_to_all(send_meta, 'dp', split_axis=0, concat_axis=0, tiled=True)]
    unnamed x35 -> x2, local copies, waits for them, and re-layouts: 0.13 us -> 3.11 us
  transfers between devices with their start and end apart: 4 -> 0, of which waited for: 4 -> 0; matrix products, arithmetic and copies ran while one was open for 3% -> 0% of each run, Pallas kernels for 0% -> 0%
where the time goes in v1:
time: 72.8 us; the launch traced here: 72.6 us
  Pallas kernels  68.9 us (95%)
  local copies, waits for them, and re-layouts  3.11 us (4%)
    pallas_call x1, Pallas kernels, body(): pl.pallas_call(functools.partial(kernel, groups, tensors), out_shape=(jax...  68.9 us
    unnamed x2, local copies, waits for them, and re-layouts  3.11 us

profile of v1, /device:TPU:0, one launch (start us, length us, event | category | flops | bytes accessed | tf_op | source)
XLA Modules:
  0.0 72.6 jit_solution(8269856467648041080)
XLA Ops:
  0.6 68.9 %shard_map.176 = (bf16[512,128]{1,0:T(8,128)(2,1)}, bf16[48,1024]{1,0:T(8,128)(2,1)}) custom-call(bf16[512,1024]{1,0:T(8,128)(2,1)} %residues.1, s32[4]{0:T(128)} %block_protein.1, s32[16]{0:T(128)} %protein_length.1, s32[16]{0:T(128)} %decoder_group.1, f32[1,1024]{1,0:T(1,128)} %bitcast.4, bf16[1024,1024]{1,0:T(8,128)(2,1)} %enc_query.1, ...), custom_call_target="tpu_custom_call" | custom-call | tf_op jit(solution)/shard_map/pallas_call | solution.py:562
  69.5 1.6 %copy.21 = bf16[512,128]{1,0:T(8,128)(2,1)} copy(bf16[512,128]{1,0:T(8,128)(2,1)} %get-tuple-element.4) | data formatting | bytes 262144
  71.1 1.5 %copy.22 = bf16[48,1024]{1,0:T(8,128)(2,1)} copy(bf16[48,1024]{1,0:T(8,128)(2,1)} %get-tuple-element.5) | data formatting | bytes 196608

commit v2 on v1

--- a/solution.py
+++ b/solution.py
@@ -15,7 +15,8 @@
 LOG2E = 1.4426950408889634
 MASKED = -1000000000.0
 SCORE_SCALE = HEAD_DIM ** (-0.5)
-RAW_MASKED = MASKED / SCORE_SCALE
+QUERY_SCALE = SCORE_SCALE * LOG2E
+RAW_MASKED = MASKED * LOG2E
 MESH = pl.DeviceIdType.MESH
 F32 = jnp.float32
 BF16 = jnp.bfloat16
@@ -28,35 +29,83 @@
         target[start : start + rows, :] = (values * scale * gain[...]).astype(BF16)
 
 
-def project(source, weight, target, tile=256):
+def project(source, weight, target, scale=None, tile=512):
     @pl.loop(0, weight.shape[1] // tile)
     def _(index):
         columns = pl.ds(pl.multiple_of(index * tile, tile), tile)
-        target[:, columns] = jnp.dot(
-            source[...], weight[:, columns], preferred_element_type=F32
-        ).astype(BF16)
+        sums = jnp.dot(source[...], weight[:, columns], preferred_element_type=F32)
+        if scale is not None:
+            sums = sums * scale
+        target[:, columns] = sums.astype(BF16)
+
+
+def project_values(source, weight, target, scale=None, tile=512):
+    @pl.loop(0, weight.shape[1] // tile)
+    def _(index):
+        columns = pl.ds(pl.multiple_of(index * tile, tile), tile)
+        sums = jnp.dot(source[...], weight[:, columns], preferred_element_type=F32)
+        if scale is not None:
+            sums = sums * scale
+        for head in range(tile // HEAD_DIM):
+            start = pl.multiple_of(index * 2 * tile + head * 2 * HEAD_DIM, 2 * HEAD_DIM)
+            target[:, pl.ds(start, HEAD_DIM)] = sums[
+                :, head * HEAD_DIM : (head + 1) * HEAD_DIM
+            ].astype(BF16)
+
+
+def fill_ones(target):
+    ones = jnp.ones((target.shape[0], HEAD_DIM), BF16)
+    for start in range(HEAD_DIM, target.shape[1], 2 * HEAD_DIM):
+        target[:, start : start + HEAD_DIM] = ones
+
+
+def raw_scores(queries, keys):
+    return lax.dot_general(
+        queries, keys, (((1,), (1,)), ((), ())), preferred_element_type=F32
+    )
 
 
 def attend(queries, keys, values, bias, context, q_rows, k_rows, heads, together=2):
     @pl.loop(0, heads // together)
     def _(index):
         for inner in range(together):
-            start = pl.multiple_of((index * together + inner) * HEAD_DIM, HEAD_DIM)
-            columns = pl.ds(start, HEAD_DIM)
-            scores = lax.dot_general(
-                queries[q_rows, columns],
-                keys[k_rows, columns],
-                (((1,), (1,)), ((), ())),
-                preferred_element_type=F32,
-            )
-            scores = scores + bias[...]
-            top = jnp.max(scores, axis=1, keepdims=True)
-            expo = jnp.exp2((scores - top) * (SCORE_SCALE * LOG2E))
-            total = jnp.sum(expo, axis=1, keepdims=True)
+            head = index * together + inner
+            columns = pl.ds(pl.multiple_of(head * HEAD_DIM, HEAD_DIM), HEAD_DIM)
+            both = pl.ds(pl.multiple_of(head * 2 * HEAD_DIM, HEAD_DIM), 2 * HEAD_DIM)
+            scores = raw_scores(queries[q_rows, columns], keys[k_rows, columns]) + bias[...]
+            expo = jnp.exp2(scores - jnp.max(scores, axis=1, keepdims=True))
             mixed = jnp.dot(
-                expo.astype(BF16), values[k_rows, columns], preferred_element_type=F32
-            )
-            context[q_rows, columns] = (mixed / total).astype(BF16)
+                expo.astype(BF16), values[k_rows, both], preferred_element_type=F32
+            )
+            context[q_rows, columns] = (mixed[:, :HEAD_DIM] / mixed[:, HEAD_DIM:]).astype(BF16)
+
+
+def attend_part(queries, keys, values, bias, tops, sums, context, heads, first, last, together=2):
+    spread = keys.shape[0] // HEAD_DIM
+
+    @pl.loop(0, heads // together)
+    def _(index):
+        for inner in range(together):
+            head = index * together + inner
+            columns = pl.ds(pl.multiple_of(head * HEAD_DIM, HEAD_DIM), HEAD_DIM)
+            both = pl.ds(pl.multiple_of(head * 2 * HEAD_DIM, HEAD_DIM), 2 * HEAD_DIM)
+            scores = raw_scores(queries[:, columns], keys[:, columns]) + bias[...]
+            top = jnp.broadcast_to(
+                jnp.max(scores, axis=1, keepdims=True), (scores.shape[0], HEAD_DIM)
+            )
+            if not first:
+                before = tops[head]
+                top = jnp.maximum(top, before)
+            expo = jnp.exp2(scores - jnp.concatenate([top] * spread, axis=1))
+            mixed = jnp.dot(expo.astype(BF16), values[:, both], preferred_element_type=F32)
+            if not first:
+                decay = jnp.exp2(before - top)
+                mixed = mixed + sums[head] * jnp.concatenate([decay] * 2, axis=1)
+            if last:
+                context[:, columns] = (mixed[:, :HEAD_DIM] / mixed[:, HEAD_DIM:]).astype(BF16)
+            else:
+                tops[head] = top
+                sums[head] = mixed
 
 
 def kernel(
@@ -111,6 +160,8 @@
     c_v,
     c_ctx,
     c_bias,
+    c_tops,
+    c_sums,
     scaled,
     dpart,
     drx1,
@@ -245,9 +296,14 @@
 
     loads[0].wait()
     normalise(res_v, enc_gain, normed, BLOCK)
-    for index, (weight, target) in enumerate(((w_eq, e_q), (w_ek, e_k), (w_ev, e_v))):
-        loads[1 + index].wait()
-        project(normed, weight, target)
+    fill_ones(e_v)
+    fill_ones(c_v)
+    loads[1].wait()
+    project(normed, w_eq, e_q, QUERY_SCALE)
+    loads[2].wait()
+    project(normed, w_ek, e_k)
+    loads[3].wait()
+    project_values(normed, w_ev, e_v)
 
     block_lane = lax.broadcasted_iota(jnp.int32, (BLOCK, BLOCK), 1)
 
@@ -313,7 +369,7 @@
             normalise(dec_v, dec_gain, d_normed, BLOCK)
             second_stage(0)
     loads[6].wait()
-    project(d_normed, w_cq, c_q)
+    project(d_normed, w_cq, c_q, QUERY_SCALE)
     second_stage(1)
 
     for step in range(1, groups):
@@ -423,14 +479,20 @@
                 values * final_gain[:, j * share : (j + 1) * share]
             ).astype(BF16)
         key_scale = lax.rsqrt(squares / width + EPSILON)
-        rows = pl.ds(g * slot_rows, slot_rows)
-        for weight, target in ((w_ck, c_k), (w_cv, c_v)):
-
-            @pl.loop(0, weight.shape[1] // 256)
-            def _(index):
-                columns = pl.ds(pl.multiple_of(index * 256, 256), 256)
-                sums = jnp.dot(scaled[...], weight[:, columns], preferred_element_type=F32)
-                target[rows, columns] = (sums * key_scale).astype(BF16)
+        project(scaled, w_ck, c_k, key_scale)
+        project_values(scaled, w_cv, c_v, key_scale)
+        attend_part(
+            c_q,
+            c_k,
+            c_v,
+            c_bias.at[:, pl.ds(g * slot_rows, slot_rows)],
+            c_tops,
+            c_sums,
+            c_ctx,
+            heads,
+            g == 0,
+            g == groups - 1,
+        )
 
     loads[7].wait()
     loads[8].wait()
@@ -442,18 +504,6 @@
             forward(g - 1)
         if g >= 2:
             keys_values(g - 2)
-
-    attend(
-        c_q,
-        c_k,
-        c_v,
-        c_bias,
-        c_ctx,
-        pl.ds(0, query_rows),
-        pl.ds(0, groups * slot_rows),
-        heads,
-        2 if groups * slot_rows <= 1024 else 1,
-    )
 
     loads[9].wait()
     half_width = width // 2
@@ -518,6 +568,17 @@
 
     for copy in sent:
         copy.wait_send()
+
+
+def hand_over(first, second, first_out, second_out, sems):
+    copies = [
+        pltpu.make_async_copy(first, first_out, sems.at[0]),
+        pltpu.make_async_copy(second, second_out, sems.at[1]),
+    ]
+    for copy in copies:
+        copy.start()
+    for copy in copies:
+        copy.wait()
 
 
 def body(groups, tensors, *args):
@@ -559,7 +620,7 @@
     weight = pltpu.VMEM((width, inner), BF16)
     out_weight = pltpu.VMEM((inner, width), BF16)
     dma = pltpu.SemaphoreType.DMA
-    return pl.pallas_call(
+    results = pl.pallas_call(
         functools.partial(kernel, groups, tensors),
         out_shape=(
             jax.ShapeDtypeStruct((tok_rows, share), BF16),
@@ -599,7 +660,7 @@
             pltpu.VMEM((tok_rows, width), BF16),
             pltpu.VMEM((tok_rows, inner), BF16),
             pltpu.VMEM((tok_rows, inner), BF16),
-            pltpu.VMEM((tok_rows, inner), BF16),
+            pltpu.VMEM((tok_rows, 2 * inner), BF16),
             pltpu.VMEM((tok_rows, inner), BF16),
             pltpu.VMEM((2, half, key_span), F32),
             pltpu.VMEM((2, 2, pairs, half, share), BF16),
@@ -612,10 +673,12 @@
             pltpu.VMEM((groups, 8, LANES), jnp.int32),
             pltpu.VMEM((query_rows, width), BF16),
             pltpu.VMEM((query_rows, inner), BF16),
-            pltpu.VMEM((keys, inner), BF16),
-            pltpu.VMEM((keys, inner), BF16),
+            pltpu.VMEM((slot_rows, inner), BF16),
+            pltpu.VMEM((slot_rows, 2 * inner), BF16),
             pltpu.VMEM((query_rows, inner), BF16),
             pltpu.VMEM((query_rows, keys), F32),
+            pltpu.VMEM((inner // HEAD_DIM, query_rows, HEAD_DIM), F32),
+            pltpu.VMEM((inner // HEAD_DIM, query_rows, 2 * HEAD_DIM), F32),
             pltpu.VMEM((slot_rows, width), BF16),
             pltpu.VMEM((2, 2, pairs, row_pad, width // 2), BF16),
             pltpu.VMEM((2, pairs, row_pad, width // 2), BF16),
@@ -657,6 +720,16 @@
     )
 
 
+    return pl.pallas_call(
+        hand_over,
+        out_shape=tuple(jax.ShapeDtypeStruct(r.shape, r.dtype) for r in results),
+        in_specs=[hbm, hbm],
+        out_specs=(hbm, hbm),
+        scratch_shapes=[dma((2,))],
+        compiler_params=pltpu.CompilerParams(vmem_limit_bytes=60 * 1024 * 1024),
+    )(*results)
+
+
 def solution(mesh):
     in_specs = (
         P("dp", None),

time: 72.8 us -> 73.6 us (1.011)
  Pallas kernels: 68.9 us -> 72.8 us
  local copies, waits for them, and re-layouts: 3.11 us -> 0 us
    pallas_call x0 -> x1, Pallas kernels: none -> 8.07 us  [body(): pl.pallas_call(hand_over, out_shape=tuple((jax.ShapeDtypeStruct(r.shape,...]
    pallas_call x1, Pallas kernels: 68.9 us -> 64.7 us  [body(): pl.pallas_call(functools.partial(kernel, groups, tensors), out_shape=(jax...]
    unnamed x2 -> x0, local copies, waits for them, and re-layouts: 3.11 us -> none
where the time goes in v2:
time: 73.6 us; the launch traced here: 73.4 us
  Pallas kernels  72.8 us (99%)
    pallas_call x1, Pallas kernels, body(): pl.pallas_call(functools.partial(kernel, groups, tensors), out_shape=(jax...  64.7 us
    pallas_call x1, Pallas kernels, body(): pl.pallas_call(hand_over, out_shape=tuple((jax.ShapeDtypeStruct(r.shape,...  8.07 us

profile of v2, /device:TPU:0, one launch (start us, length us, event | category | flops | bytes accessed | tf_op | source)
XLA Modules:
  0.0 73.4 jit_solution(15538857957090683533)
XLA Ops:
  0.6 64.7 %shard_map.176 = (bf16[512,128]{1,0:T(8,128)(2,1)}, bf16[48,1024]{1,0:T(8,128)(2,1)}) custom-call(bf16[512,1024]{1,0:T(8,128)(2,1)} %residues.1, s32[4]{0:T(128)} %block_protein.1, s32[16]{0:T(128)} %protein_length.1, s32[16]{0:T(128)} %decoder_group.1, f32[1,1024]{1,0:T(1,128)} %bitcast.4, bf16[1024,1024]{1,0:T(8,128)(2,1)} %enc_query.1, ...), custom_call_target="tpu_custom_call" | custom-call | tf_op jit(solution)/shard_map/pallas_call | solution.py:623
  65.4 8.1 %shard_map.177 = (bf16[512,128]{1,0:T(8,128)(2,1)}, bf16[48,1024]{1,0:T(8,128)(2,1)}) custom-call(bf16[512,128]{1,0:T(8,128)(2,1)} %get-tuple-element.4.first, bf16[48,1024]{1,0:T(8,128)(2,1)} %get-tuple-element.5.second), custom_call_target="tpu_custom_call" | custom-call | tf_op jit(solution)/shard_map/pallas_call | solution.py:723

commit v3 on v2

--- a/solution.py
+++ b/solution.py
@@ -30,9 +30,8 @@
 
 
 def project(source, weight, target, scale=None, tile=512):
-    @pl.loop(0, weight.shape[1] // tile)
-    def _(index):
-        columns = pl.ds(pl.multiple_of(index * tile, tile), tile)
+    for start in range(0, weight.shape[1], tile):
+        columns = slice(start, start + tile)
         sums = jnp.dot(source[...], weight[:, columns], preferred_element_type=F32)
         if scale is not None:
             sums = sums * scale
@@ -40,17 +39,15 @@
 
 
 def project_values(source, weight, target, scale=None, tile=512):
-    @pl.loop(0, weight.shape[1] // tile)
-    def _(index):
-        columns = pl.ds(pl.multiple_of(index * tile, tile), tile)
-        sums = jnp.dot(source[...], weight[:, columns], preferred_element_type=F32)
+    for start in range(0, weight.shape[1], tile):
+        sums = jnp.dot(
+            source[...], weight[:, start : start + tile], preferred_element_type=F32
+        )
         if scale is not None:
             sums = sums * scale
-        for head in range(tile // HEAD_DIM):
-            start = pl.multiple_of(index * 2 * tile + head * 2 * HEAD_DIM, 2 * HEAD_DIM)
-            target[:, pl.ds(start, HEAD_DIM)] = sums[
-                :, head * HEAD_DIM : (head + 1) * HEAD_DIM
-            ].astype(BF16)
+        for inner in range(0, tile, HEAD_DIM):
+            place = 2 * (start + inner)
+            target[:, place : place + HEAD_DIM] = sums[:, inner : inner + HEAD_DIM].astype(BF16)
 
 
 def fill_ones(target):
@@ -65,47 +62,66 @@
     )
 
 
-def attend(queries, keys, values, bias, context, q_rows, k_rows, heads, together=2):
-    @pl.loop(0, heads // together)
-    def _(index):
-        for inner in range(together):
-            head = index * together + inner
-            columns = pl.ds(pl.multiple_of(head * HEAD_DIM, HEAD_DIM), HEAD_DIM)
-            both = pl.ds(pl.multiple_of(head * 2 * HEAD_DIM, HEAD_DIM), 2 * HEAD_DIM)
-            scores = raw_scores(queries[q_rows, columns], keys[k_rows, columns]) + bias[...]
-            expo = jnp.exp2(scores - jnp.max(scores, axis=1, keepdims=True))
-            mixed = jnp.dot(
-                expo.astype(BF16), values[k_rows, both], preferred_element_type=F32
-            )
-            context[q_rows, columns] = (mixed[:, :HEAD_DIM] / mixed[:, HEAD_DIM:]).astype(BF16)
-
-
-def attend_part(queries, keys, values, bias, tops, sums, context, heads, first, last, together=2):
+def head_columns(group, together):
+    single, double = [], []
+    for inner in range(together):
+        head = group * together + inner
+        single.append(slice(head * HEAD_DIM, (head + 1) * HEAD_DIM))
+        double.append(slice(2 * head * HEAD_DIM, 2 * (head + 1) * HEAD_DIM))
+    return list(zip(single, double))
+
+
+def attend(queries, keys, values, bias, context, q_rows, k_rows, heads, together=4):
+    for group in range(heads // together):
+        places = head_columns(group, together)
+        scores = [
+            raw_scores(queries[q_rows, one], keys[k_rows, one]) + bias[...] for one, _ in places
+        ]
+        weights = [
+            jnp.exp2(one - jnp.max(one, axis=1, keepdims=True)).astype(BF16) for one in scores
+        ]
+        mixed = [
+            jnp.dot(weight, values[k_rows, two], preferred_element_type=F32)
+            for weight, (_, two) in zip(weights, places)
+        ]
+        for value, (one, _) in zip(mixed, places):
+            context[q_rows, one] = (value[:, :HEAD_DIM] / value[:, HEAD_DIM:]).astype(BF16)
+
+
+def attend_part(queries, keys, values, bias, tops, sums, context, heads, first, last, together=4):
     spread = keys.shape[0] // HEAD_DIM
-
-    @pl.loop(0, heads // together)
-    def _(index):
-        for inner in range(together):
-            head = index * together + inner
-            columns = pl.ds(pl.multiple_of(head * HEAD_DIM, HEAD_DIM), HEAD_DIM)
-            both = pl.ds(pl.multiple_of(head * 2 * HEAD_DIM, HEAD_DIM), 2 * HEAD_DIM)
-            scores = raw_scores(queries[:, columns], keys[:, columns]) + bias[...]
-            top = jnp.broadcast_to(
-                jnp.max(scores, axis=1, keepdims=True), (scores.shape[0], HEAD_DIM)
-            )
-            if not first:
-                before = tops[head]
-                top = jnp.maximum(top, before)
-            expo = jnp.exp2(scores - jnp.concatenate([top] * spread, axis=1))
-            mixed = jnp.dot(expo.astype(BF16), values[:, both], preferred_element_type=F32)
-            if not first:
-                decay = jnp.exp2(before - top)
-                mixed = mixed + sums[head] * jnp.concatenate([decay] * 2, axis=1)
+    for group in range(heads // together):
+        places = head_columns(group, together)
+        base = group * together
+        scores = [raw_scores(queries[:, one], keys[:, one]) + bias[...] for one, _ in places]
+        highest = [
+            jnp.broadcast_to(jnp.max(one, axis=1, keepdims=True), (one.shape[0], HEAD_DIM))
+            for one in scores
+        ]
+        if not first:
+            before = [tops[base + inner] for inner in range(together)]
+            highest = [jnp.maximum(a, b) for a, b in zip(highest, before)]
+        weights = [
+            jnp.exp2(one - jnp.concatenate([top] * spread, axis=1)).astype(BF16)
+            for one, top in zip(scores, highest)
+        ]
+        mixed = [
+            jnp.dot(weight, values[:, two], preferred_element_type=F32)
+            for weight, (_, two) in zip(weights, places)
+        ]
+        if not first:
+            decays = [jnp.exp2(b - a) for a, b in zip(highest, before)]
+            mixed = [
+                value + sums[base + inner] * jnp.concatenate([decays[inner]] * 2, axis=1)
+                for inner, value in enumerate(mixed)
+            ]
+        for inner, (one, _) in enumerate(places):
+            value = mixed[inner]
             if last:
-                context[:, columns] = (mixed[:, :HEAD_DIM] / mixed[:, HEAD_DIM:]).astype(BF16)
+                context[:, one] = (value[:, :HEAD_DIM] / value[:, HEAD_DIM:]).astype(BF16)
             else:
-                tops[head] = top
-                sums[head] = mixed
+                tops[base + inner] = highest[inner]
+                sums[base + inner] = value
 
 
 def kernel(
@@ -283,6 +299,17 @@
             ids = jnp.where(lane < row_live, slot_id, ids)
         meta_tx[g] = ids
 
+    fill_ones(e_v)
+    fill_ones(c_v)
+    loads[0].wait()
+    normalise(res_v, enc_gain, normed, BLOCK)
+    loads[1].wait()
+    project(normed, w_eq, e_q, QUERY_SCALE)
+    loads[2].wait()
+    project(normed, w_ek, e_k)
+    loads[3].wait()
+    project_values(normed, w_ev, e_v)
+
     pl.semaphore_wait(barrier, 1 + (pairs - 1) + (groups - 1))
     for step in range(1, groups):
         target = lax.rem(me_dp + step, groups)
@@ -293,17 +320,6 @@
             {"dp": target},
         )
     meta_rx[0] = meta_tx[me_dp]
-
-    loads[0].wait()
-    normalise(res_v, enc_gain, normed, BLOCK)
-    fill_ones(e_v)
-    fill_ones(c_v)
-    loads[1].wait()
-    project(normed, w_eq, e_q, QUERY_SCALE)
-    loads[2].wait()
-    project(normed, w_ek, e_k)
-    loads[3].wait()
-    project_values(normed, w_ev, e_v)
 
     block_lane = lax.broadcasted_iota(jnp.int32, (BLOCK, BLOCK), 1)
 
@@ -417,7 +433,7 @@
                 chosen = jnp.where(match, 1.0, 0.0)
                 block = block + chosen * encoded[b * BLOCK : (b + 1) * BLOCK, :].astype(F32)
             placed[g, s * BLOCK : (s + 1) * BLOCK, :] = block.astype(BF16)
-    for step in range(1, groups):
+    for step in range(groups - 1, 0, -1):
         target = lax.rem(me_dp + step, groups)
         send(
             placed.at[target],
@@ -570,15 +586,9 @@
         copy.wait_send()
 
 
-def hand_over(first, second, first_out, second_out, sems):
-    copies = [
-        pltpu.make_async_copy(first, first_out, sems.at[0]),
-        pltpu.make_async_copy(second, second_out, sems.at[1]),
-    ]
-    for copy in copies:
-        copy.start()
-    for copy in copies:
-        copy.wait()
+def hand_over(first, second, first_out, second_out):
+    first_out[...] = first[...]
+    second_out[...] = second[...]
 
 
 def body(groups, tensors, *args):
@@ -723,9 +733,8 @@
     return pl.pallas_call(
         hand_over,
         out_shape=tuple(jax.ShapeDtypeStruct(r.shape, r.dtype) for r in results),
-        in_specs=[hbm, hbm],
-        out_specs=(hbm, hbm),
-        scratch_shapes=[dma((2,))],
+        in_specs=[vmem, vmem],
+        out_specs=(vmem, vmem),
         compiler_params=pltpu.CompilerParams(vmem_limit_bytes=60 * 1024 * 1024),
     )(*results)
 

time: 73.6 us -> 53.4 us (0.73)
  Pallas kernels: 72.8 us -> 52.6 us
    pallas_call x1, Pallas kernels: 64.7 us -> 51 us  [body(): pl.pallas_call(functools.partial(kernel, groups, tensors), out_shape=(jax...]
    pallas_call x1, Pallas kernels: 8.07 us -> 1.65 us  [body(): pl.pallas_call(hand_over, out_shape=tuple((jax.ShapeDtypeStruct(r.shape,...]
where the time goes in v3:
time: 53.4 us; the launch traced here: 53.3 us
  Pallas kernels  52.6 us (99%)
  between operations  0.65 us (1%)
    pallas_call x1, Pallas kernels, body(): pl.pallas_call(functools.partial(kernel, groups, tensors), out_shape=(jax...  51 us
    pallas_call x1, Pallas kernels, body(): pl.pallas_call(hand_over, out_shape=tuple((jax.ShapeDtypeStruct(r.shape,...  1.65 us

profile of v3, /device:TPU:0, one launch (start us, length us, event | category | flops | bytes accessed | tf_op | source)
XLA Modules:
  0.0 53.3 jit_solution(9950484889565077106)
XLA Ops:
  0.6 51.0 %shard_map.176 = (bf16[512,128]{1,0:T(8,128)(2,1)}, bf16[48,1024]{1,0:T(8,128)(2,1)}) custom-call(bf16[512,1024]{1,0:T(8,128)(2,1)} %residues.1, s32[4]{0:T(128)} %block_protein.1, s32[16]{0:T(128)} %protein_length.1, s32[16]{0:T(128)} %decoder_group.1, f32[1,1024]{1,0:T(1,128)} %bitcast.4, bf16[1024,1024]{1,0:T(8,128)(2,1)} %enc_query.1, ...), custom_call_target="tpu_custom_call" | custom-call | tf_op jit(solution)/shard_map/pallas_call | solution.py:633
  51.6 1.7 %shard_map.177 = (bf16[512,128]{1,0:T(8,128)(2,1)}, bf16[48,1024]{1,0:T(8,128)(2,1)}) custom-call(bf16[512,128]{1,0:T(8,128)(2,1)} %get-tuple-element.4.first, bf16[48,1024]{1,0:T(8,128)(2,1)} %get-tuple-element.5.second), custom_call_target="tpu_custom_call" | custom-call | tf_op jit(solution)/shard_map/pallas_call | solution.py:733
